TPU v7x, 32 devices: a whole 2x2x4 slice. The times are simulated.
32 devices in a mesh: groups: 2 (over y), ctx: 4 (over z), head: 4 (over x, core).
Axes of the slice: x: 2, y: 2, z: 4, core: 2. Of those that a mesh axis runs over, the one named last changes fastest.
Arguments:
- tokens: bfloat16 [4096, 4096], P(('groups', 'ctx')), parts along dimension 0, may hold values from -14 to 14
- lengths: int32 [32], P('groups'), parts along dimension 0, may hold values from 1 to 1024, 2048 in all
- q_weight: bfloat16 [4096, 4096], P(None, 'head'), may hold values from -21 to 21
- k_weight: bfloat16 [4096, 1024], P(None, 'head'), may hold values from -7 to 7
- v_weight: bfloat16 [4096, 1024], P(None, 'head'), may hold values from -0.09375 to 0.09375
- o_weight: bfloat16 [4096, 4096], P('head'), may hold values from -0.5 to 0.5
Outputs:
- mixed: bfloat16 [4096, 4096], P(('groups', 'ctx'), 'head'), parts along dimension 0
There are 2 independent parts, one for each index of `groups`. A program takes and returns all parts, laid end to end along the dimension named above; an argument that names none is the same for every part. Nothing has to cross between parts.
Inputs may be any that keep to these rules, and one draw needn't show every extreme that they name: lengths sum to 2048, and the longest document has exactly 1024 tokens.
All inputs are finite; a program needn't handle non-finite values.
Results may differ from a plain program's by a relative error of at most 0.017.
Values may be sent and summed in bfloat16 or wider, within the bound.
A program may use at most 320 MiB of HBM per device.

v0:
```python
import math

import jax
import jax.numpy as jnp
from jax import lax
from jax.sharding import PartitionSpec as P

HD = 128


def fold_positions(rows, shard_rows, shard_count):
    shard = rows // shard_rows
    inner = rows % shard_rows
    half_rows = shard_rows // 2
    block = jnp.where(inner < half_rows, shard, 2 * shard_count - 1 - shard)
    return block * half_rows + inner % half_rows


def doc_info(place, lengths):
    ends = jnp.cumsum(lengths)
    passed = ends[None, :] <= place[:, None]
    document = jnp.sum(passed.astype(jnp.int32), axis=1)
    first = jnp.sum(jnp.where(passed, lengths[None, :], 0), axis=1)
    return (document, first)


def rotate(values, offset):
    half_size = values.shape[-1] // 2
    expo = jnp.arange(half_size).astype(jnp.float32) * (2.0 / values.shape[-1])
    inverse = jnp.exp(-math.log(500000.0) * expo)
    angle = offset.astype(jnp.float32)[:, None] * inverse[None, :]
    cosine = jnp.cos(angle)[:, None, :]
    sine = jnp.sin(angle)[:, None, :]
    left = values[..., :half_size]
    right = values[..., half_size:]
    return jnp.concatenate([left * cosine - right * sine, right * cosine + left * sine], axis=-1)


def rms_norm(tokens):
    wide = tokens.astype(jnp.float32)
    scale = lax.rsqrt(jnp.mean(wide * wide, axis=-1, keepdims=True) + 1e-05)
    return (wide * scale).astype(jnp.bfloat16)


def shards(tokens, lengths, q_weight, k_weight, v_weight, o_weight):
    shard_rows = tokens.shape[0]
    shard_count = lax.axis_size("ctx")
    device = lax.axis_index("ctx")
    rows = device * shard_rows + jnp.arange(shard_rows, dtype=jnp.int32)
    place = fold_positions(rows, shard_rows, shard_count)
    document, first = doc_info(place, lengths)
    offset = place - first
    normed = rms_norm(tokens)
    query_heads = q_weight.shape[1] // HD
    kv_heads = k_weight.shape[1] // HD
    group = query_heads // kv_heads
    query = rotate(
        jnp.dot(normed, q_weight, preferred_element_type=jnp.float32).reshape(
            shard_rows, query_heads, HD
        ),
        offset,
    ).astype(jnp.bfloat16)
    query = query.reshape(shard_rows, kv_heads, group, HD)
    keys = rotate(
        jnp.dot(normed, k_weight, preferred_element_type=jnp.float32).reshape(
            shard_rows, kv_heads, HD
        ),
        offset,
    ).astype(jnp.bfloat16)
    values = jnp.dot(normed, v_weight, preferred_element_type=jnp.float32).astype(jnp.bfloat16)
    stacked = jnp.stack([keys.reshape(shard_rows, kv_heads * HD), values])
    scale = 1.0 / math.sqrt(HD)
    piece = lax.all_gather(stacked, "ctx", axis=1, tiled=True)
    count = piece.shape[1]
    key_rows = jnp.arange(count, dtype=jnp.int32)
    key_place = fold_positions(key_rows, shard_rows, shard_count)
    key_doc, unused = doc_info(key_place, lengths)
    allowed = (
        (key_doc[None, :] == document[:, None]) & (key_place[None, :] <= place[:, None]) & True
    )
    maxima = jnp.full((kv_heads, group, shard_rows), -1e30, jnp.float32)
    key_block = piece[0].reshape(count, kv_heads, HD)
    value_block = piece[1].reshape(count, kv_heads, HD)
    scores = (
        jnp.einsum("tkgd,skd->kgts", query, key_block, preferred_element_type=jnp.float32) * scale
    )
    scores = jnp.where(allowed, scores, -1e30)
    fresh = jnp.maximum(maxima, jnp.max(scores, axis=-1))
    expo = jnp.where(allowed, jnp.exp(scores - fresh[..., None]), 0.0)
    totals = jnp.sum(expo, axis=-1)
    accum = jnp.einsum(
        "kgts,skd->kgtd", expo.astype(jnp.bfloat16), value_block, preferred_element_type=jnp.float32
    )
    carry = (fresh, totals, accum)
    maxima, totals, accum = carry
    heads_out = (accum / totals[..., None]).astype(jnp.bfloat16)
    projection = o_weight.reshape(kv_heads, group, HD, o_weight.shape[1])
    partial_value = jnp.einsum(
        "kgtd,kgde->te", heads_out, projection, preferred_element_type=jnp.float32
    )
    summed = lax.psum_scatter(
        partial_value.astype(jnp.bfloat16), "head", scatter_dimension=1, tiled=True
    )
    return summed


def solution(mesh):
    return jax.shard_map(
        shards,
        mesh=mesh,
        in_specs=(
            P(("groups", "ctx"), None),
            P("groups"),
            P(None, "head"),
            P(None, "head"),
            P(None, "head"),
            P("head", None),
        ),
        out_specs=P(("groups", "ctx"), "head"),
        check_vma=False,
    )
```

profile of v0, /device:TPU:24, one launch (start us, length us, event | category | flops | bytes accessed | tf_op | source)
XLA Modules:
  0.0 171.6 jit_solution(7145825207817683527)
XLA Ops:
  6.6 3.2 %fusion.5 = f32[512]{0:T(512)S(1)} fusion(bf16[512,4096]{1,0:T(8,128)(2,1)} %param.6), kind=kLoop, calls=%fused_computation.9 | loop fusion | flops 6290944 | bytes 4196352 | tf_op jit(solution)/shard_map/reduce_sum | solution.py:41
  9.8 0.1 copy.34
  9.9 0.1 reduce
  10.1 0.1 fusion.26
  10.2 0.0 copy-start.2
  10.2 3.6 %fusion.11 = bf16[1,512,256]{2,1,0:T(8,128)(2,1)S(1)} fusion(bf16[4096,256]{1,0:T(8,128)(2,1)S(1)} %copy-done, bf16[512,4096]{1,0:T(8,128)(2,1)} %param.6, f32[512]{0:T(512)S(1)} %add_rsqrt_fusion), kind=kOutput, calls=%fused_computation.20 | convolution fusion | flops 1080164352 | bytes 6555648 | tf_op jit(solution)/shard_map/dot_general | solution.py:70
  13.9 0.5 copy-done.5
  14.3 1.7 fusion.47
  16.0 0.5 multiply_cosine_fusion
  16.5 0.1 subtract_convert_fusion.1
  16.7 0.1 copy.48
  16.8 0.8 pad_maximum_fusion
  17.7 0.0 all-gather.2.cloned.1.call-update
  17.7 0.2 reduce-scatter.2.cloned.1.call-start
  17.9 0.1 copy.36
  18.0 0.1 copy.37
  18.2 8.2 %convolution_bitcast_fusion = f32[64,8,8,128]{3,1,2,0:T(8,128)S(1)} fusion(bf16[4096,1024]{1,0:T(8,128)(2,1)} %param.8, bf16[512,4096]{1,0:T(8,128)(2,1)} %param.6, f32[512]{0:T(512)S(1)} %add_rsqrt_fusion), kind=kOutput, calls=%fused_computation.18 | convolution fusion | flops 4301258752 | bytes 14682112 | tf_op jit(solution)/shard_map/dot_general | solution.py:58
  26.4 0.5 copy.52
  26.9 0.9 subtract_convert_fusion
  27.8 1.2 copy.38
  28.9 1.1 copy.39
  30.1 0.1 convert_reduce_fusion
  30.2 1.6 compare_and_fusion
  31.7 30.8 %all-gather.2.cloned.1.call-done = bf16[2,2048,256]{2,1,0:T(8,128)(2,1)} async-done(((bf16[2,512,256]{2,1,0:T(8,128)(2,1)}), bf16[2,2048,256]{2,1,0:T(8,128)(2,1)}) %all-gather.2.cloned.1.call-update) | async-done | bytes 2097168 | tf_op jit(solution)/shard_map/all_gather | solution.py:73
  62.6 1.7 fusion.49
  64.2 1.1 reshape_squeeze.7
  65.4 0.3 reshape_squeeze.6
  65.6 15.9 %fusion = (f32[2,4,512]{2,1,0:T(4,128)S(1)}, f32[2,2048,512,4]{2,1,3,0:T(8,128)}) fusion(pred[512,2048]{0,1:T(8,128)(4,1)S(1)} %compare_and_fusion, bf16[512,2,4,64]{3,0,2,1:T(8,128)(2,1)} %bitcast.35, bf16[512,2,4,64]{3,0,2,1:T(8,128)(2,1)} %bitcast.34, bf16[2048,2,128,1]{2,1,0,3:T(2,128)(2,1)S(1)} %bitcast.36), kind=kOutput, calls=%fused_computation.2 | convolution fusion | flops 2174742528 | bytes 36716544 | tf_op jit(solution)/shard_map/tkgd,skd->kgts/dot_general | solution.py:85
  81.6 21.0 %fusion.1 = (f32[2,4,512]{2,1,0:T(4,128)S(1)}, bf16[2,4,512,2048]{2,3,1,0:T(8,128)(2,1)}) fusion(f32[2,2048,512,4]{2,1,3,0:T(8,128)} %get-tuple-element.18, f32[2,4,512]{2,1,0:T(4,128)S(1)} %broadcast_maximum_fusion, pred[512,2048]{0,1:T(8,128)(4,1)S(1)} %compare_and_fusion), kind=kLoop, calls=%fused_computation.3 | loop fusion | flops 50327552 | bytes 51412992 | tf_op jit(solution)/shard_map/reduce_sum | solution.py:90
  102.6 16.6 %bitcast_convert_fusion = bf16[512,4096]{1,0:T(8,128)(2,1)} fusion(bf16[2,4,128,4096]{3,2,1,0:T(8,128)(2,1)} %bitcast.40, bf16[2,4,512,2048]{2,3,1,0:T(8,128)(2,1)} %get-tuple-element.8, bf16[2048,2,128]{2,1,0:T(2,128)(2,1)S(1)} %copy-done.3, f32[2,4,512]{2,0,1:T(2,128)S(1)} %copy.43), kind=kOutput, calls=%fused_computation.11 | convolution fusion | flops 6445596672 | bytes 30425088 | tf_op jit(solution)/shard_map/kgtd,kgde->te/dot_general | solution.py:98
  119.2 0.0 reduce-scatter.2.cloned.1.call-update
  119.2 45.6 %reduce-scatter.2.cloned.1.call-done = bf16[512,1024]{1,0:T(8,128)(2,1)} async-done(((bf16[512,4096]{1,0:T(8,128)(2,1)}), bf16[512,1024]{1,0:T(8,128)(2,1)}) %reduce-scatter.2.cloned.1.call-update) | async-done | bytes 1048592 | tf_op jit(solution)/shard_map/reduce_scatter | solution.py:101
  (20 shorter events, 0.2 us)
Async XLA Ops:
  6.5 3.6 %copy-start = (bf16[4096,256]{1,0:T(8,128)(2,1)S(1)}, bf16[4096,256]{1,0:T(8,128)(2,1)}, u32[]{:S(2)}) copy-start(bf16[4096,256]{1,0:T(8,128)(2,1)} %param.10) | copy-start | bytes 6291460
  6.5 3.3 %copy-start.4 = (s32[16]{0:T(128)S(1)}, s32[16]{0:T(128)}, u32[]{:S(2)}) copy-start(s32[16]{0:T(128)} %param.7) | copy-start | bytes 196
  6.5 56.0 %all-gather.2.cloned.1.call-start = ((), (), s32[]{:S(2)}) async-start(), calls=%async_computation.1 | async-start | bytes 2621440 | tf_op jit(solution)/shard_map/all_gather | solution.py:73
  10.2 3.7 %copy-start.2 = (bf16[512,4096]{1,0:T(8,128)(2,1)S(1)}, bf16[512,4096]{1,0:T(8,128)(2,1)}, u32[]{:S(2)}) copy-start(bf16[512,4096]{1,0:T(8,128)(2,1)} %param.6) | copy-start | bytes 12582916
  10.2 4.1 %copy-start.5 = (bf16[4096,256]{1,0:T(8,128)(2,1)S(1)}, bf16[4096,256]{1,0:T(8,128)(2,1)}, u32[]{:S(2)}) copy-start(bf16[4096,256]{1,0:T(8,128)(2,1)} %param.9) | copy-start | bytes 6291460
  17.7 147.1 %reduce-scatter.2.cloned.1.call-start = ((), (), s32[]{:S(2)}) async-start(), calls=%async_computation.2 | async-start | bytes 5242880 | tf_op jit(solution)/shard_map/reduce_scatter | solution.py:101
  81.6 21.0 %copy-start.3 = (bf16[2048,2,128]{2,1,0:T(2,128)(2,1)S(1)}, bf16[2048,2,128]{2,1,0:T(2,128)(2,1)}, u32[]{:S(2)}) copy-start(bf16[2048,2,128]{2,1,0:T(2,128)(2,1)} %reshape_squeeze.7) | copy-start | bytes 3145732
  102.6 62.2 %copy-start.1 = (bf16[4096,256]{1,0:T(8,128)(2,1)S(1)}, bf16[4096,256]{1,0:T(8,128)(2,1)}, u32[]{:S(2)}) copy-start(bf16[4096,256]{1,0:T(8,128)(2,1)} %param.10) | copy-start | bytes 6291460
Sparse Core Ops, SparseCore 0:
  17.8 44.7 all-gather.1
  119.4 45.3 reduce-scatter.1
where the time goes:
time: 174 us; the launch traced here: 172 us
  waiting for transfers between devices  76.4 us (44%)
  matrix products  46.1 us (26%)
  other arithmetic  28.5 us (16%)
  between operations  13.6 us (8%)
  local copies, waits for them, and re-layouts  6.81 us (4%)
    reduce_scatter x1, waiting for transfers between devices, shards(): lax.psum_scatter(partial_value.astype(jnp.bfloat16), 'head', scatter_dime...  45.6 us
    all_gather x1, waiting for transfers between devices, shards(): piece = lax.all_gather(stacked, 'ctx', axis=1, tiled=True)  30.8 us
    reduce_sum x1, other arithmetic, shards(): totals = jnp.sum(expo, axis=-1)  21 us
    dot_general x1, matrix products, shards(): jnp.einsum('kgtd,kgde->te', heads_out, projection, preferred_element_type...  16.6 us
    dot_general x1, matrix products, shards(): jnp.einsum('tkgd,skd->kgts', query, key_block, preferred_element_type=jnp...  15.9 us
    dot_general x1, matrix products, shards(): jnp.dot(normed, q_weight, preferred_element_type=jnp.float32)  8.25 us
    dot_general x1, matrix products, shards(): jnp.dot(normed, v_weight, preferred_element_type=jnp.float32)  3.62 us
  transfers between devices with their start and end apart: 2, of which 2 were waited for; matrix products, arithmetic and copies ran while one was open for 8% of the time, Pallas kernels for 0%

commit v1 on v0

v1 whole, which is shorter than its diff:
```python
import functools
import math

import jax
import jax.numpy as jnp
from jax import lax
from jax.experimental import pallas as pl
from jax.experimental.pallas import tpu as pltpu
from jax.sharding import PartitionSpec as P

HD = 128
MESH = pl.DeviceIdType.MESH
LOW = -1e30


def tables(lengths, rows, ctx_count):
    half = rows // 2
    device = lax.axis_index("ctx")
    inner = jnp.arange(rows, dtype=jnp.int32)
    block = jnp.where(inner < half, device, 2 * ctx_count - 1 - device)
    place = block * half + inner % half
    ends = jnp.cumsum(lengths)
    passed = ends[None, :] <= place[:, None]
    first = jnp.sum(jnp.where(passed, lengths[None, :], 0), axis=1)
    offset = (place - first).astype(jnp.float32)
    expo = jnp.arange(HD // 2).astype(jnp.float32) * (2.0 / HD)
    inverse = jnp.exp(-math.log(500000.0) * expo)
    angle = offset[:, None] * inverse[None, :]
    cosine, sine = jnp.cos(angle), jnp.sin(angle)
    return (
        first.astype(jnp.int32)[None, :],
        jnp.concatenate([cosine, cosine], axis=1),
        jnp.concatenate([-sine, sine], axis=1),
    )


def rotated(values, cosine, sine):
    return values * cosine + pltpu.roll(values, HD // 2, 1) * sine


def kernel(
    n, n_head, first_ref, cos_ref, sin_ref, tok_hbm, qw_hbm, kw_hbm, vw_hbm, ow_hbm,
    out_ref,
    tok, qw, kvw, ow, kv_acc, norm, query, keys, values, top, total, accum, attended,
    own, kept, sib_out, sib_in, far_out, far_in,
    tok_sem, kw_sem, vw_sem, qw_sem, ow_sem,
    kv_send, kv_recv, sib_send, sib_recv, far_send, far_recv,
):
    rows, depth = tok.shape
    half = rows // 2
    kv_heads = keys.shape[1]
    q_heads = query.shape[0]
    group = q_heads // kv_heads
    k_cols = kv_heads * HD
    chips = n_head // 2
    width = out_ref.shape[1]
    pieces = 4
    piece = depth // pieces

    c = lax.axis_index("ctx")
    head = lax.axis_index("head")
    chip, core = lax.div(head, 2), lax.rem(head, 2)
    sibling = chip * 2 + 1 - core
    has_left, has_right = c > 0, c < n - 1
    low_block, high_block = c, 2 * n - 1 - c

    def other_chip(step):
        return lax.rem(chip + step, chips)

    def load_piece(k):
        cols = pl.ds(pl.multiple_of(k * piece, piece), piece)
        return (
            pltpu.make_async_copy(tok_hbm.at[:, cols], tok.at[:, cols], tok_sem.at[k]),
            pltpu.make_async_copy(kw_hbm.at[cols, :], kvw.at[cols, 0:k_cols], kw_sem.at[k]),
            pltpu.make_async_copy(
                vw_hbm.at[cols, :], kvw.at[cols, k_cols : 2 * k_cols], vw_sem.at[k]
            ),
        )

    for k in range(pieces):
        for copy in load_piece(k):
            copy.start()
    load_q = pltpu.make_async_copy(qw_hbm, qw, qw_sem)
    load_o = pltpu.make_async_copy(ow_hbm, ow, ow_sem)

    barrier = pltpu.get_barrier_semaphore()

    def greet(target):
        pl.semaphore_signal(barrier, inc=1, device_id=target, device_id_type=MESH)

    @pl.when(has_left)
    def _():
        greet({"ctx": c - 1})

    @pl.when(has_right)
    def _():
        greet({"ctx": c + 1})

    greet({"head": sibling})
    for step in range(1, chips):
        greet({"head": other_chip(step) * 2 + core})

    kv_acc[...] = jnp.zeros_like(kv_acc)
    norm[...] = jnp.zeros_like(norm)

    def project_piece(k, carry):
        for copy in load_piece(k):
            copy.wait()
        cols = pl.ds(pl.multiple_of(k * piece, piece), piece)

        def squares(r, inner):
            at = pl.ds(pl.multiple_of(r * 64, 64), 64)
            wide = tok[at, cols].astype(jnp.float32)
            sq = wide * wide
            part = sq[:, 0:HD]
            for s in range(1, piece // HD):
                part = part + sq[:, s * HD : (s + 1) * HD]
            norm[at, :] += part
            return inner

        lax.fori_loop(0, rows // 64, squares, 0)
        kv_acc[...] += jnp.dot(tok[:, cols], kvw[cols, :], preferred_element_type=jnp.float32)
        return carry

    lax.fori_loop(0, pieces, project_piece, 0)
    load_q.start()
    load_o.start()
    mean = jnp.sum(norm[...], axis=1, keepdims=True) * (1.0 / depth)
    norm[...] = jnp.broadcast_to(lax.rsqrt(mean + 1e-05), norm.shape)
    for g in range(kv_heads):
        for side, block in ((0, low_block), (1, high_block)):
            at = slice(side * half, (side + 1) * half)
            raw = kv_acc[at, g * HD : (g + 1) * HD] * norm[at, :]
            keys[block, g] = rotated(raw, cos_ref[at, :], sin_ref[at, :]).astype(jnp.bfloat16)
            raw = kv_acc[at, k_cols + g * HD : k_cols + (g + 1) * HD] * norm[at, :]
            values[block, g] = raw.T.astype(jnp.bfloat16)

    def block_copies(block, way):
        target = {"ctx": c + 1 if way else c - 1}
        return [
            pltpu.make_async_remote_copy(
                src_ref=ref.at[block],
                dst_ref=ref.at[block],
                send_sem=kv_send.at[way, kind, block],
                recv_sem=kv_recv.at[kind, block],
                device_id=target,
                device_id_type=MESH,
            )
            for kind, ref in enumerate((keys, values))
        ]

    def send(block, way):
        for copy in block_copies(block, way):
            copy.start()

    def receive(block):
        for copy in block_copies(block, 0):
            copy.wait_recv()

    greeted = 1 + (chips - 1) + has_left.astype(jnp.int32) + has_right.astype(jnp.int32)
    pl.semaphore_wait(barrier, greeted)

    @pl.when(has_right)
    def _():
        send(low_block, 1)

    @pl.when(has_left)
    def _():
        send(high_block, 0)

    load_q.wait()
    factor = math.log2(math.e) / math.sqrt(HD)
    tile = min(256, q_heads * HD)

    def project_query(t, carry):
        cols = pl.ds(pl.multiple_of(t * tile, tile), tile)
        raw = jnp.dot(tok[...], qw[:, cols], preferred_element_type=jnp.float32)
        for h in range(tile // HD):
            part = raw[:, h * HD : (h + 1) * HD] * (norm[...] * factor)
            query[t * (tile // HD) + h] = rotated(part, cos_ref[...], sin_ref[...]).astype(
                jnp.bfloat16
            )
        return carry

    lax.fori_loop(0, q_heads * HD // tile, project_query, 0)

    def attend(side, block, diagonal):
        at = pl.ds(pl.multiple_of(side * half, half), half)

        def one_group(g, carry):
            k = keys[block, g]
            v = values[block, g]
            key_at = lax.broadcasted_iota(jnp.int32, (half, half), 0)
            allowed = key_at >= first_ref[:, at] - block * half
            if diagonal:
                allowed = allowed & (key_at <= lax.broadcasted_iota(jnp.int32, (half, half), 1))
            for j in range(group):
                h = g * group + j
                slot = side * q_heads + h
                scores = lax.dot_general(
                    k, query[h, at, :], (((1,), (1,)), ((), ())),
                    preferred_element_type=jnp.float32,
                )
                scores = jnp.where(allowed, scores, LOW)
                here = jnp.max(scores, axis=0, keepdims=True)
                if not diagonal:
                    before = top[slot]
                    here = jnp.maximum(before, here)
                expo = jnp.exp2(scores - here)
                summed = jnp.sum(expo, axis=0, keepdims=True)
                fresh = jnp.dot(v, expo.astype(jnp.bfloat16), preferred_element_type=jnp.float32)
                if not diagonal:
                    shrink = jnp.exp2(before - here)
                    summed = summed + total[slot] * shrink
                    fresh = fresh + accum[slot] * shrink
                top[slot] = here
                total[slot] = summed
                accum[slot] = fresh
            return carry

        lax.fori_loop(0, kv_heads, one_group, 0)

    def sib_copy(side, x):
        return pltpu.make_async_remote_copy(
            src_ref=sib_out.at[side, x],
            dst_ref=sib_in.at[side, x],
            send_sem=sib_send.at[side, x],
            recv_sem=sib_recv.at[side, x],
            device_id={"head": sibling},
            device_id_type=MESH,
        )

    def far_copy(side, step):
        x = other_chip(step)
        return pltpu.make_async_remote_copy(
            src_ref=far_out.at[side, step - 1],
            dst_ref=far_in.at[side, step - 1],
            send_sem=far_send.at[side, step - 1],
            recv_sem=far_recv.at[side, step - 1],
            device_id={"head": x * 2 + core},
            device_id_type=MESH,
        )

    out_tile = min(256, width)

    def project_out(owner, store):
        def one_tile(t, carry):
            start = pl.multiple_of(owner * width + t * out_tile, out_tile)
            part = jnp.dot(
                attended[...], ow[:, pl.ds(start, out_tile)], preferred_element_type=jnp.float32
            )
            store(pl.ds(pl.multiple_of(t * out_tile, out_tile), out_tile), part)
            return carry

        lax.fori_loop(0, width // out_tile, one_tile, 0)

    def finish(side):
        for h in range(q_heads):
            slot = side * q_heads + h
            result = accum[slot] / total[slot]
            attended[:, h * HD : (h + 1) * HD] = result.T.astype(jnp.bfloat16)
        for step in list(range(1, chips)) + [0]:
            x = other_chip(step)

            def to_sibling(at, part):
                sib_out[side, x, :, at] = part.astype(jnp.bfloat16)

            project_out(x * 2 + 1 - core, to_sibling)
            sib_copy(side, x).start()
        for step in range(1, chips):
            x = other_chip(step)

            def to_own(at, part):
                own[:, at] = part

            project_out(x * 2 + core, to_own)
            sib_copy(side, x).wait_recv()
            far_out[side, step - 1] = (
                own[...] + sib_in[side, x].astype(jnp.float32)
            ).astype(jnp.bfloat16)
            far_copy(side, step).start()

        def to_kept(at, part):
            kept[side, :, at] = part

        project_out(chip * 2 + core, to_kept)

    attend(0, low_block, True)
    attend(1, high_block, True)

    @pl.when(c >= n - 1 - c)
    def _():
        attend(1, low_block, False)

    load_o.wait()
    last_right = jnp.maximum(c + 1, n - 1 - c)
    right_count = jnp.where(has_right, 2 * n - 1 - c - last_right, 0)

    def turn(i, carry):
        left_block, right_block = c - i, 2 * n - 1 - c - i
        from_left = (i >= 1) & (i <= c)
        from_right = (i >= 1) & (i <= right_count)

        @pl.when(from_left)
        def _():
            receive(left_block)

            @pl.when(has_right)
            def _():
                send(left_block, 1)

        @pl.when(from_right)
        def _():
            receive(right_block)

            @pl.when(has_left & (right_block >= n - c))
            def _():
                send(right_block, 0)

        @pl.when((i == right_count) & has_left & (c >= n - c))
        def _():
            send(low_block, 0)

        @pl.when(from_left)
        def _():
            attend(0, left_block, False)

        @pl.when(i == c)
        def _():
            finish(0)

        @pl.when(from_left & (left_block >= n - 1 - c))
        def _():
            attend(1, left_block, False)

        @pl.when(from_right)
        def _():
            attend(1, right_block, False)

        return carry

    lax.fori_loop(0, n + 1, turn, 0)
    finish(1)

    for side in range(2):
        sib_copy(side, chip).wait_recv()
        mixed = kept[side] + sib_in[side, chip].astype(jnp.float32)
        for step in range(1, chips):
            far_copy(side, step).wait_recv()
            mixed = mixed + far_in[side, step - 1].astype(jnp.float32)
        out_ref[side * half : (side + 1) * half, :] = mixed.astype(jnp.bfloat16)

    for side in range(2):
        for x in range(chips):
            sib_copy(side, x).wait_send()
        for step in range(1, chips):
            far_copy(side, step).wait_send()

    def drain(block, carry):
        @pl.when(has_right & (block <= c))
        def _():
            for copy in block_copies(block, 1):
                copy.wait_send()

        @pl.when(has_left & (block >= jnp.maximum(c, n - c)) & (block <= high_block))
        def _():
            for copy in block_copies(block, 0):
                copy.wait_send()

        return carry

    lax.fori_loop(0, 2 * n, drain, 0)


def shards(n, n_head, tokens, lengths, q_weight, k_weight, v_weight, o_weight):
    rows, depth = tokens.shape
    half = rows // 2
    q_cols, k_cols = q_weight.shape[1], k_weight.shape[1]
    q_heads, kv_heads = q_cols // HD, k_cols // HD
    chips = n_head // 2
    width = o_weight.shape[1] // n_head
    first, cosine, sine = tables(lengths, rows, n)
    bf16, f32 = jnp.bfloat16, jnp.float32
    dma = pltpu.SemaphoreType.DMA
    far = max(chips - 1, 1)
    vmem = pl.BlockSpec(memory_space=pltpu.VMEM)
    hbm = pl.BlockSpec(memory_space=pl.ANY)
    return pl.pallas_call(
        functools.partial(kernel, n, n_head),
        out_shape=jax.ShapeDtypeStruct((rows, width), bf16),
        in_specs=[vmem] * 3 + [hbm] * 5,
        out_specs=vmem,
        scratch_shapes=[
            pltpu.VMEM((rows, depth), bf16),
            pltpu.VMEM((depth, q_cols), bf16),
            pltpu.VMEM((depth, 2 * k_cols), bf16),
            pltpu.VMEM(o_weight.shape, bf16),
            pltpu.VMEM((rows, 2 * k_cols), f32),
            pltpu.VMEM((rows, HD), f32),
            pltpu.VMEM((q_heads, rows, HD), bf16),
            pltpu.VMEM((2 * n, kv_heads, half, HD), bf16),
            pltpu.VMEM((2 * n, kv_heads, HD, half), bf16),
            pltpu.VMEM((2 * q_heads, 1, half), f32),
            pltpu.VMEM((2 * q_heads, 1, half), f32),
            pltpu.VMEM((2 * q_heads, HD, half), f32),
            pltpu.VMEM((half, q_cols), bf16),
            pltpu.VMEM((half, width), f32),
            pltpu.VMEM((2, half, width), f32),
            pltpu.VMEM((2, chips, half, width), bf16),
            pltpu.VMEM((2, chips, half, width), bf16),
            pltpu.VMEM((2, far, half, width), bf16),
            pltpu.VMEM((2, far, half, width), bf16),
            dma((4,)), dma((4,)), dma((4,)), dma, dma,
            dma((2, 2, 2 * n)), dma((2, 2 * n)),
            dma((2, chips)), dma((2, chips)),
            dma((2, far)), dma((2, far)),
        ],
        compiler_params=pltpu.CompilerParams(
            collective_id=0, has_side_effects=True, vmem_limit_bytes=60 * 2**20
        ),
    )(first, cosine, sine, tokens, q_weight, k_weight, v_weight, o_weight)


def solution(mesh):
    return jax.shard_map(
        functools.partial(shards, mesh.shape["ctx"], mesh.shape["head"]),
        mesh=mesh,
        in_specs=(
            P(("groups", "ctx"), None),
            P("groups"),
            P(None, "head"),
            P(None, "head"),
            P(None, "head"),
            P("head", None),
        ),
        out_specs=P(("groups", "ctx"), "head"),
        check_vma=False,
    )
```

time: 174 us -> 75.8 us (0.44); the launches traced: 172 us -> 75.6 us
  waiting for transfers between devices: 76.4 us -> 0 us
  Pallas kernels: 0 us -> 69.7 us
  matrix products: 46.1 us -> 0 us
  other arithmetic: 28.5 us -> 2.92 us
  between operations: 13.6 us -> 0.03 us
  local copies, waits for them, and re-layouts: 6.81 us -> 3 us
    pallas_call x0 -> x1, Pallas kernels: none -> 69.7 us  [shards(): pl.pallas_call(functools.partial(kernel, n, n_head), out_shape=jax.ShapeD...]
    dot_general x5 -> x0, matrix products: 46.1 us -> none  [the longest x1 16.6 us: shards(): jnp.einsum('kgtd,kgde->te', heads_out, projection, preferred_element_type...]
    reduce_scatter x1 -> x0, waiting for transfers between devices: 45.6 us -> none  [shards(): lax.psum_scatter(partial_value.astype(jnp.bfloat16), 'head', scatter_dime...]
    all_gather x1 -> x0, waiting for transfers between devices: 30.8 us -> none  [shards(): piece = lax.all_gather(stacked, 'ctx', axis=1, tiled=True)]
    reduce_sum x4 -> x1, other arithmetic: 24.4 us -> 0.74 us  [tables(): first = jnp.sum(jnp.where(passed, lengths[None, :], 0), axis=1)]
    another operation x5 -> x1, local copies, waits for them, and re-layouts: 3.78 us -> 0.74 us
    another operation x6 -> x2, other arithmetic: 1.96 us -> 0.15 us
  transfers between devices with their start and end apart: 2 -> 0, of which waited for: 2 -> 0; matrix products, arithmetic and copies ran while one was open for 8% -> 0% of each run, Pallas kernels for 0% -> 0%
where the time goes in v1:
time: 75.8 us; the launch traced here: 75.6 us
  Pallas kernels  69.7 us (92%)
  local copies, waits for them, and re-layouts  3 us (4%)
  other arithmetic  2.92 us (4%)
    pallas_call x1, Pallas kernels, shards(): pl.pallas_call(functools.partial(kernel, n, n_head), out_shape=jax.ShapeD...  69.7 us
    unnamed x3, local copies, waits for them, and re-layouts  2.27 us

profile of v1, /device:TPU:24, one launch (start us, length us, event | category | flops | bytes accessed | tf_op | source)
XLA Modules:
  0.0 75.6 jit_solution(1179187598542175908)
XLA Ops:
  0.0 0.7 copy.9
  0.8 0.1 reduce
  0.9 0.7 select_reduce_fusion
  1.6 0.0 copy-start
  1.7 1.0 %fusion = (f32[512,64]{1,0:T(8,128)S(1)}, f32[512,64]{1,0:T(8,128)S(1)}, f32[512,64]{1,0:T(8,128)S(1)}) fusion(f32[64]{0:T(128)S(1)} %multiply_exponential_fusion, f32[512]{0:T(512)S(1)} %subtract_convert_fusion), kind=kLoop, calls=%fused_computation.4 | loop fusion | flops 65536 | bytes 395520 | tf_op jit(solution)/shard_map/neg | solution.py:33
  2.7 1.0 %pad_maximum_fusion = (f32[512,128]{1,0:T(8,128)}, f32[512,128]{1,0:T(8,128)}) fusion(f32[512,64]{1,0:T(8,128)S(1)} %get-tuple-element.7, f32[512,64]{1,0:T(8,128)S(1)} %get-tuple-element.6, f32[512,64]{1,0:T(8,128)S(1)} %get-tuple-element.5), kind=kLoop, calls=%fused_computation.2 | loop fusion | flops 131072 | bytes 917504 | tf_op jit(solution)/shard_map/concatenate | solution.py:32
  3.7 0.0 copy-done
  3.7 69.7 %shard_map.64 = bf16[512,1024]{1,0:T(8,128)(2,1)} custom-call(s32[1,512]{1,0:T(1,128)} %bitcast.2, f32[512,128]{1,0:T(8,128)} %get-tuple-element.8.cos_ref, f32[512,128]{1,0:T(8,128)} %get-tuple-element.9.sin_ref, bf16[512,4096]{1,0:T(8,128)(2,1)} %tok_hbm.1, bf16[4096,1024]{1,0:T(8,128)(2,1)} %qw_hbm.1, bf16[4096,256]{1,0:T(8,128)(2,1)} %kw_hbm.1, ...), custom_call_target="tpu_custom_call" | custom-call | tf_op jit(solution)/shard_map/pallas_call | solution.py:388
  73.3 2.3 %copy.11 = bf16[512,1024]{1,0:T(8,128)(2,1)} copy(bf16[512,1024]{1,0:T(8,128)(2,1)} %shard_map.64) | data formatting | bytes 2097152
  (4 shorter events, 0.1 us)
Async XLA Ops:
  1.6 2.0 %copy-start = (s32[512]{0:T(512)}, s32[512]{0:T(512)S(1)}, u32[]{:S(2)}) copy-start(s32[512]{0:T(512)S(1)} %select_reduce_fusion) | copy-start | bytes 6148

commit v2 on v1

--- a/solution.py
+++ b/solution.py
@@ -13,35 +13,14 @@
 LOW = -1e30
 
 
-def tables(lengths, rows, ctx_count):
-    half = rows // 2
-    device = lax.axis_index("ctx")
-    inner = jnp.arange(rows, dtype=jnp.int32)
-    block = jnp.where(inner < half, device, 2 * ctx_count - 1 - device)
-    place = block * half + inner % half
-    ends = jnp.cumsum(lengths)
-    passed = ends[None, :] <= place[:, None]
-    first = jnp.sum(jnp.where(passed, lengths[None, :], 0), axis=1)
-    offset = (place - first).astype(jnp.float32)
-    expo = jnp.arange(HD // 2).astype(jnp.float32) * (2.0 / HD)
-    inverse = jnp.exp(-math.log(500000.0) * expo)
-    angle = offset[:, None] * inverse[None, :]
-    cosine, sine = jnp.cos(angle), jnp.sin(angle)
-    return (
-        first.astype(jnp.int32)[None, :],
-        jnp.concatenate([cosine, cosine], axis=1),
-        jnp.concatenate([-sine, sine], axis=1),
-    )
-
-
 def rotated(values, cosine, sine):
     return values * cosine + pltpu.roll(values, HD // 2, 1) * sine
 
 
 def kernel(
-    n, n_head, first_ref, cos_ref, sin_ref, tok_hbm, qw_hbm, kw_hbm, vw_hbm, ow_hbm,
+    n, n_head, lengths_ref, tok_hbm, qw_hbm, kw_hbm, vw_hbm, ow_hbm,
     out_ref,
-    tok, qw, kvw, ow, kv_acc, norm, query, keys, values, top, total, accum, attended,
+    first_ref, cos_ref, sin_ref, tok, qw, kvw, ow, kv_acc, norm, query, keys, values, top, total, accum, attended,
     own, kept, sib_out, sib_in, far_out, far_in,
     tok_sem, kw_sem, vw_sem, qw_sem, ow_sem,
     kv_send, kv_recv, sib_send, sib_recv, far_send, far_recv,
@@ -49,8 +28,9 @@
     rows, depth = tok.shape
     half = rows // 2
     kv_heads = keys.shape[1]
-    q_heads = query.shape[0]
-    group = q_heads // kv_heads
+    group = query.shape[2] // half
+    q_heads = kv_heads * group
+    wide_rows = group * half
     k_cols = kv_heads * HD
     chips = n_head // 2
     width = out_ref.shape[1]
@@ -99,6 +79,32 @@
     greet({"head": sibling})
     for step in range(1, chips):
         greet({"head": other_chip(step) * 2 + core})
+
+    def starts(place):
+        first, end = jnp.zeros_like(place), 0
+        for d in range(lengths_ref.shape[0]):
+            end = end + lengths_ref[d]
+            first = jnp.where(place >= end, end, first)
+        return first
+
+    for side, block in ((0, low_block), (1, high_block)):
+        lane = lax.broadcasted_iota(jnp.int32, (1, half), 1)
+        row_first = starts(block * half + lane)
+        first_ref[side] = jnp.concatenate([row_first] * group, axis=1)
+    lane = lax.broadcasted_iota(jnp.int32, (half, HD), 1)
+    on_left = lane < HD // 2
+    place = jnp.where(on_left, low_block, high_block) * half + lax.broadcasted_iota(
+        jnp.int32, (half, HD), 0
+    )
+    offset = (place - starts(place)).astype(jnp.float32)
+    expo = (lane % (HD // 2)).astype(jnp.float32) * (2.0 / HD)
+    angle = offset * jnp.exp(-math.log(500000.0) * expo)
+    cosine, sine = jnp.cos(angle), jnp.sin(angle)
+    cosine_over, sine_over = pltpu.roll(cosine, HD // 2, 1), pltpu.roll(sine, HD // 2, 1)
+    cos_ref[0:half, :] = jnp.where(on_left, cosine, cosine_over)
+    cos_ref[half:rows, :] = jnp.where(on_left, cosine_over, cosine)
+    sin_ref[0:half, :] = jnp.where(on_left, -sine, sine_over)
+    sin_ref[half:rows, :] = jnp.where(on_left, -sine_over, sine)
 
     kv_acc[...] = jnp.zeros_like(kv_acc)
     norm[...] = jnp.zeros_like(norm)
@@ -177,45 +183,45 @@
         raw = jnp.dot(tok[...], qw[:, cols], preferred_element_type=jnp.float32)
         for h in range(tile // HD):
             part = raw[:, h * HD : (h + 1) * HD] * (norm[...] * factor)
-            query[t * (tile // HD) + h] = rotated(part, cos_ref[...], sin_ref[...]).astype(
-                jnp.bfloat16
+            turned = rotated(part, cos_ref[...], sin_ref[...]).astype(jnp.bfloat16)
+            at_head = t * (tile // HD) + h
+            g, j = lax.div(at_head, group), lax.rem(at_head, group)
+            at = pl.ds(pl.multiple_of(j * half, half), half)
+            for side in range(2):
+                query[g, side, at, :] = turned[side * half : (side + 1) * half]
+        return carry
+
+    lax.fori_loop(0, q_heads * HD // tile, project_query, 0)
+
+    def attend(side, block, diagonal):
+        def one_group(g, carry):
+            slot = side * kv_heads + g
+            key_at = lax.broadcasted_iota(jnp.int32, (half, wide_rows), 0)
+            allowed = key_at >= first_ref[side] - block * half
+            if diagonal:
+                row_at = lax.broadcasted_iota(jnp.int32, (1, wide_rows), 1) % half
+                allowed = allowed & (key_at <= row_at)
+            scores = lax.dot_general(
+                keys[block, g], query[g, side], (((1,), (1,)), ((), ())),
+                preferred_element_type=jnp.float32,
             )
-        return carry
-
-    lax.fori_loop(0, q_heads * HD // tile, project_query, 0)
-
-    def attend(side, block, diagonal):
-        at = pl.ds(pl.multiple_of(side * half, half), half)
-
-        def one_group(g, carry):
-            k = keys[block, g]
-            v = values[block, g]
-            key_at = lax.broadcasted_iota(jnp.int32, (half, half), 0)
-            allowed = key_at >= first_ref[:, at] - block * half
-            if diagonal:
-                allowed = allowed & (key_at <= lax.broadcasted_iota(jnp.int32, (half, half), 1))
-            for j in range(group):
-                h = g * group + j
-                slot = side * q_heads + h
-                scores = lax.dot_general(
-                    k, query[h, at, :], (((1,), (1,)), ((), ())),
-                    preferred_element_type=jnp.float32,
-                )
-                scores = jnp.where(allowed, scores, LOW)
-                here = jnp.max(scores, axis=0, keepdims=True)
-                if not diagonal:
-                    before = top[slot]
-                    here = jnp.maximum(before, here)
-                expo = jnp.exp2(scores - here)
-                summed = jnp.sum(expo, axis=0, keepdims=True)
-                fresh = jnp.dot(v, expo.astype(jnp.bfloat16), preferred_element_type=jnp.float32)
-                if not diagonal:
-                    shrink = jnp.exp2(before - here)
-                    summed = summed + total[slot] * shrink
-                    fresh = fresh + accum[slot] * shrink
-                top[slot] = here
-                total[slot] = summed
-                accum[slot] = fresh
+            scores = jnp.where(allowed, scores, LOW)
+            here = jnp.max(scores, axis=0, keepdims=True)
+            if not diagonal:
+                before = top[slot]
+                here = jnp.maximum(before, here)
+            expo = jnp.exp2(scores - here)
+            summed = jnp.sum(expo, axis=0, keepdims=True)
+            fresh = jnp.dot(
+                values[block, g], expo.astype(jnp.bfloat16), preferred_element_type=jnp.float32
+            )
+            if not diagonal:
+                shrink = jnp.exp2(before - here)
+                summed = summed + total[slot] * shrink
+                fresh = fresh + accum[slot] * shrink
+            top[slot] = here
+            total[slot] = summed
+            accum[slot] = fresh
             return carry
 
         lax.fori_loop(0, kv_heads, one_group, 0)
@@ -255,87 +261,105 @@
         lax.fori_loop(0, width // out_tile, one_tile, 0)
 
     def finish(side):
-        for h in range(q_heads):
-            slot = side * q_heads + h
-            result = accum[slot] / total[slot]
-            attended[:, h * HD : (h + 1) * HD] = result.T.astype(jnp.bfloat16)
+        for g in range(kv_heads):
+            slot = side * kv_heads + g
+            result = accum[slot] * (1.0 / total[slot])
+            for j in range(group):
+                h = g * group + j
+                part = result[:, j * half : (j + 1) * half]
+                attended[:, h * HD : (h + 1) * HD] = part.T.astype(jnp.bfloat16)
         for step in list(range(1, chips)) + [0]:
             x = other_chip(step)
 
             def to_sibling(at, part):
                 sib_out[side, x, :, at] = part.astype(jnp.bfloat16)
 
+            def to_own(at, part):
+                if step:
+                    own[:, at] = part
+                else:
+                    kept[side, :, at] = part
+
             project_out(x * 2 + 1 - core, to_sibling)
             sib_copy(side, x).start()
-        for step in range(1, chips):
-            x = other_chip(step)
-
-            def to_own(at, part):
-                own[:, at] = part
-
             project_out(x * 2 + core, to_own)
-            sib_copy(side, x).wait_recv()
-            far_out[side, step - 1] = (
-                own[...] + sib_in[side, x].astype(jnp.float32)
-            ).astype(jnp.bfloat16)
-            far_copy(side, step).start()
-
-        def to_kept(at, part):
-            kept[side, :, at] = part
-
-        project_out(chip * 2 + core, to_kept)
-
-    attend(0, low_block, True)
-    attend(1, high_block, True)
-
-    @pl.when(c >= n - 1 - c)
-    def _():
-        attend(1, low_block, False)
+            if step:
+                sib_copy(side, x).wait_recv()
+                far_out[side, step - 1] = (
+                    own[...] + sib_in[side, x].astype(jnp.float32)
+                ).astype(jnp.bfloat16)
+                far_copy(side, step).start()
 
     load_o.wait()
     last_right = jnp.maximum(c + 1, n - 1 - c)
     right_count = jnp.where(has_right, 2 * n - 1 - c - last_right, 0)
 
-    def turn(i, carry):
-        left_block, right_block = c - i, 2 * n - 1 - c - i
-        from_left = (i >= 1) & (i <= c)
-        from_right = (i >= 1) & (i <= right_count)
-
-        @pl.when(from_left)
-        def _():
-            receive(left_block)
+    def from_left(i):
+        return (i >= 1) & (i <= c)
+
+    def from_right(i):
+        return (i >= 1) & (i <= right_count)
+
+    def passes_right(i):
+        return from_left(i) & has_right
+
+    def passes_left(i):
+        return from_right(i) & has_left & (2 * n - 1 - c - i >= n - c)
+
+    def arrive(i):
+        @pl.when(from_left(i))
+        def _():
+            receive(c - i)
 
             @pl.when(has_right)
             def _():
-                send(left_block, 1)
-
-        @pl.when(from_right)
-        def _():
-            receive(right_block)
-
-            @pl.when(has_left & (right_block >= n - c))
+                send(c - i, 1)
+
+        @pl.when(from_right(i))
+        def _():
+            receive(2 * n - 1 - c - i)
+
+            @pl.when(passes_left(i))
             def _():
-                send(right_block, 0)
+                send(2 * n - 1 - c - i, 0)
 
         @pl.when((i == right_count) & has_left & (c >= n - c))
         def _():
             send(low_block, 0)
 
-        @pl.when(from_left)
-        def _():
-            attend(0, left_block, False)
+    arrive(0)
+
+    def turn(i, carry):
+        early = passes_right(i + 1) | passes_left(i + 1)
+
+        @pl.when(early)
+        def _():
+            arrive(i + 1)
+
+        @pl.when(i == 0)
+        def _():
+            attend(0, low_block, True)
+            attend(1, high_block, True)
+
+        @pl.when(from_left(i))
+        def _():
+            attend(0, c - i, False)
 
         @pl.when(i == c)
         def _():
             finish(0)
 
-        @pl.when(from_left & (left_block >= n - 1 - c))
-        def _():
-            attend(1, left_block, False)
-
-        @pl.when(from_right)
-        def _():
-            attend(1, right_block, False)
+        @pl.when((i <= c) & (c - i >= n - 1 - c))
+        def _():
+            attend(1, c - i, False)
+
+        @pl.when(from_right(i))
+        def _():
+            attend(1, 2 * n - 1 - c - i, False)
+
+        @pl.when(jnp.logical_not(early))
+        def _():
+            arrive(i + 1)
 
         return carry
 
@@ -379,7 +403,7 @@
     q_heads, kv_heads = q_cols // HD, k_cols // HD
     chips = n_head // 2
     width = o_weight.shape[1] // n_head
-    first, cosine, sine = tables(lengths, rows, n)
+    group = q_heads // kv_heads
     bf16, f32 = jnp.bfloat16, jnp.float32
     dma = pltpu.SemaphoreType.DMA
     far = max(chips - 1, 1)
@@ -388,21 +412,24 @@
     return pl.pallas_call(
         functools.partial(kernel, n, n_head),
         out_shape=jax.ShapeDtypeStruct((rows, width), bf16),
-        in_specs=[vmem] * 3 + [hbm] * 5,
+        in_specs=[pl.BlockSpec(memory_space=pltpu.SMEM)] + [hbm] * 5,
         out_specs=vmem,
         scratch_shapes=[
+            pltpu.VMEM((2, 1, group * half), jnp.int32),
+            pltpu.VMEM((rows, HD), f32),
+            pltpu.VMEM((rows, HD), f32),
             pltpu.VMEM((rows, depth), bf16),
             pltpu.VMEM((depth, q_cols), bf16),
             pltpu.VMEM((depth, 2 * k_cols), bf16),
             pltpu.VMEM(o_weight.shape, bf16),
             pltpu.VMEM((rows, 2 * k_cols), f32),
             pltpu.VMEM((rows, HD), f32),
-            pltpu.VMEM((q_heads, rows, HD), bf16),
+            pltpu.VMEM((kv_heads, 2, group * half, HD), bf16),
             pltpu.VMEM((2 * n, kv_heads, half, HD), bf16),
             pltpu.VMEM((2 * n, kv_heads, HD, half), bf16),
-            pltpu.VMEM((2 * q_heads, 1, half), f32),
-            pltpu.VMEM((2 * q_heads, 1, half), f32),
-            pltpu.VMEM((2 * q_heads, HD, half), f32),
+            pltpu.VMEM((2 * kv_heads, 1, group * half), f32),
+            pltpu.VMEM((2 * kv_heads, 1, group * half), f32),
+            pltpu.VMEM((2 * kv_heads, HD, group * half), f32),
             pltpu.VMEM((half, q_cols), bf16),
             pltpu.VMEM((half, width), f32),
             pltpu.VMEM((2, half, width), f32),
@@ -418,7 +445,7 @@
         compiler_params=pltpu.CompilerParams(
             collective_id=0, has_side_effects=True, vmem_limit_bytes=60 * 2**20
         ),
-    )(first, cosine, sine, tokens, q_weight, k_weight, v_weight, o_weight)
+    )(lengths, tokens, q_weight, k_weight, v_weight, o_weight)
 
 
 def solution(mesh):

time: 75.8 us -> 67.1 us (0.89)
  the two profiles are of different devices: /device:TPU:24 before, /device:TPU:0 now
where the time goes in v2:
time: 67.1 us; the launch traced here: 67 us
  Pallas kernels  64.7 us (96%)
  local copies, waits for them, and re-layouts  2.26 us (3%)
    pallas_call x1, Pallas kernels, shards(): pl.pallas_call(functools.partial(kernel, n, n_head), out_shape=jax.ShapeD...  64.7 us
    unnamed x1, local copies, waits for them, and re-layouts  2.26 us

profile of v2, /device:TPU:0, one launch (start us, length us, event | category | flops | bytes accessed | tf_op | source)
XLA Modules:
  0.0 67.0 jit_solution(1594259910710074884)
XLA Ops:
  0.0 64.7 %shard_map.64 = bf16[512,1024]{1,0:T(8,128)(2,1)} custom-call(s32[16]{0:T(128)} %lengths_ref.1, bf16[512,4096]{1,0:T(8,128)(2,1)} %tok_hbm.1, bf16[4096,1024]{1,0:T(8,128)(2,1)} %qw_hbm.1, bf16[4096,256]{1,0:T(8,128)(2,1)} %kw_hbm.1, bf16[4096,256]{1,0:T(8,128)(2,1)} %vw_hbm.1, bf16[1024,4096]{1,0:T(8,128)(2,1)} %ow_hbm.1), custom_call_target="tpu_custom_call" | custom-call | tf_op jit(solution)/shard_map/pallas_call | solution.py:412
  64.7 2.3 %copy.8 = bf16[512,1024]{1,0:T(8,128)(2,1)} copy(bf16[512,1024]{1,0:T(8,128)(2,1)} %shard_map.64) | data formatting | bytes 2097152

commit v3 on v2

--- a/solution.py
+++ b/solution.py
@@ -21,9 +21,9 @@
     n, n_head, lengths_ref, tok_hbm, qw_hbm, kw_hbm, vw_hbm, ow_hbm,
     out_ref,
     first_ref, cos_ref, sin_ref, tok, qw, kvw, ow, kv_acc, norm, query, keys, values, top, total, accum, attended,
-    own, kept, sib_out, sib_in, far_out, far_in,
+    kept, mixed, sib_out, sib_in, far_out, far_in,
     tok_sem, kw_sem, vw_sem, qw_sem, ow_sem,
-    kv_send, kv_recv, sib_send, sib_recv, far_send, far_recv,
+    kv_send, kv_recv, sib_send, sib_recv, far_send, far_recv, out_sem,
 ):
     rows, depth = tok.shape
     half = rows // 2
@@ -114,18 +114,14 @@
             copy.wait()
         cols = pl.ds(pl.multiple_of(k * piece, piece), piece)
 
-        def squares(r, inner):
-            at = pl.ds(pl.multiple_of(r * 64, 64), 64)
-            wide = tok[at, cols].astype(jnp.float32)
+        kv_acc[...] += jnp.dot(tok[:, cols], kvw[cols, :], preferred_element_type=jnp.float32)
+        for r in range(0, rows, 64):
+            wide = tok[r : r + 64, cols].astype(jnp.float32)
             sq = wide * wide
             part = sq[:, 0:HD]
             for s in range(1, piece // HD):
                 part = part + sq[:, s * HD : (s + 1) * HD]
-            norm[at, :] += part
-            return inner
-
-        lax.fori_loop(0, rows // 64, squares, 0)
-        kv_acc[...] += jnp.dot(tok[:, cols], kvw[cols, :], preferred_element_type=jnp.float32)
+            norm[r : r + 64, :] += part
         return carry
 
     lax.fori_loop(0, pieces, project_piece, 0)
@@ -159,9 +155,14 @@
         for copy in block_copies(block, way):
             copy.start()
 
-    def receive(block):
-        for copy in block_copies(block, 0):
-            copy.wait_recv()
+    def receive(block, passes, way):
+        landing, onward = block_copies(block, 0), block_copies(block, way)
+        for kind in range(2):
+            landing[kind].wait_recv()
+
+            @pl.when(passes)
+            def _():
+                onward[kind].start()
 
     greeted = 1 + (chips - 1) + has_left.astype(jnp.int32) + has_right.astype(jnp.int32)
     pl.semaphore_wait(barrier, greeted)
@@ -226,39 +227,35 @@
 
         lax.fori_loop(0, kv_heads, one_group, 0)
 
-    def sib_copy(side, x):
+    def sib_copy(side, x, t):
         return pltpu.make_async_remote_copy(
-            src_ref=sib_out.at[side, x],
-            dst_ref=sib_in.at[side, x],
-            send_sem=sib_send.at[side, x],
-            recv_sem=sib_recv.at[side, x],
+            src_ref=sib_out.at[side, x, t],
+            dst_ref=sib_in.at[side, x, t],
+            send_sem=sib_send.at[side, x, t],
+            recv_sem=sib_recv.at[side, x, t],
             device_id={"head": sibling},
             device_id_type=MESH,
         )
 
-    def far_copy(side, step):
+    def far_copy(side, step, t):
         x = other_chip(step)
         return pltpu.make_async_remote_copy(
-            src_ref=far_out.at[side, step - 1],
-            dst_ref=far_in.at[side, step - 1],
-            send_sem=far_send.at[side, step - 1],
-            recv_sem=far_recv.at[side, step - 1],
+            src_ref=far_out.at[side, step - 1, t],
+            dst_ref=far_in.at[side, step - 1, t],
+            send_sem=far_send.at[side, step - 1, t],
+            recv_sem=far_recv.at[side, step - 1, t],
             device_id={"head": x * 2 + core},
             device_id_type=MESH,
         )
 
-    out_tile = min(256, width)
-
-    def project_out(owner, store):
-        def one_tile(t, carry):
-            start = pl.multiple_of(owner * width + t * out_tile, out_tile)
-            part = jnp.dot(
-                attended[...], ow[:, pl.ds(start, out_tile)], preferred_element_type=jnp.float32
-            )
-            store(pl.ds(pl.multiple_of(t * out_tile, out_tile), out_tile), part)
-            return carry
-
-        lax.fori_loop(0, width // out_tile, one_tile, 0)
+    out_tile = sib_out.shape[4]
+    out_tiles = sib_out.shape[2]
+
+    def project_out(owner, t):
+        start = pl.multiple_of(owner * width + t * out_tile, out_tile)
+        return jnp.dot(
+            attended[...], ow[:, pl.ds(start, out_tile)], preferred_element_type=jnp.float32
+        )
 
     def finish(side):
         for g in range(kv_heads):
@@ -271,24 +268,25 @@
         for step in list(range(1, chips)) + [0]:
             x = other_chip(step)
 
-            def to_sibling(at, part):
-                sib_out[side, x, :, at] = part.astype(jnp.bfloat16)
-
-            def to_own(at, part):
+            def for_sibling(t, carry):
+                sib_out[side, x, t] = project_out(x * 2 + 1 - core, t).astype(jnp.bfloat16)
+                sib_copy(side, x, t).start()
+                return carry
+
+            def for_own(t, carry):
+                part = project_out(x * 2 + core, t)
                 if step:
-                    own[:, at] = part
+                    sib_copy(side, x, t).wait_recv()
+                    far_out[side, step - 1, t] = (
+                        part + sib_in[side, x, t].astype(jnp.float32)
+                    ).astype(jnp.bfloat16)
+                    far_copy(side, step, t).start()
                 else:
-                    kept[side, :, at] = part
-
-            project_out(x * 2 + 1 - core, to_sibling)
-            sib_copy(side, x).start()
-            project_out(x * 2 + core, to_own)
-            if step:
-                sib_copy(side, x).wait_recv()
-                far_out[side, step - 1] = (
-                    own[...] + sib_in[side, x].astype(jnp.float32)
-                ).astype(jnp.bfloat16)
-                far_copy(side, step).start()
+                    kept[side, t] = part
+                return carry
+
+            lax.fori_loop(0, out_tiles, for_sibling, 0)
+            lax.fori_loop(0, out_tiles, for_own, 0)
 
     load_o.wait()
     last_right = jnp.maximum(c + 1, n - 1 - c)
@@ -306,22 +304,17 @@
     def passes_left(i):
         return from_right(i) & has_left & (2 * n - 1 - c - i >= n - c)
 
+    last_pass = jnp.where(has_left, jnp.minimum(right_count, n - 1), 0)
+    finish_turn = jnp.maximum(c, jnp.where(c < n - c, last_pass, right_count) - 1)
+
     def arrive(i):
         @pl.when(from_left(i))
         def _():
-            receive(c - i)
-
-            @pl.when(has_right)
-            def _():
-                send(c - i, 1)
+            receive(c - i, has_right, 1)
 
         @pl.when(from_right(i))
         def _():
-            receive(2 * n - 1 - c - i)
-
-            @pl.when(passes_left(i))
-            def _():
-                send(2 * n - 1 - c - i, 0)
+            receive(2 * n - 1 - c - i, passes_left(i), 0)
 
         @pl.when((i == right_count) & has_left & (c >= n - c))
         def _():
@@ -345,7 +338,7 @@
         def _():
             attend(0, c - i, False)
 
-        @pl.when(i == c)
+        @pl.when(i == finish_turn)
         def _():
             finish(0)
 
@@ -366,19 +359,35 @@
     lax.fori_loop(0, n + 1, turn, 0)
     finish(1)
 
+    def result_copy(side, t):
+        cols = pl.ds(pl.multiple_of(t * out_tile, out_tile), out_tile)
+        at = slice(side * half, (side + 1) * half)
+        return pltpu.make_async_copy(mixed.at[side, t], out_ref.at[at, cols], out_sem.at[side, t])
+
     for side in range(2):
-        sib_copy(side, chip).wait_recv()
-        mixed = kept[side] + sib_in[side, chip].astype(jnp.float32)
-        for step in range(1, chips):
-            far_copy(side, step).wait_recv()
-            mixed = mixed + far_in[side, step - 1].astype(jnp.float32)
-        out_ref[side * half : (side + 1) * half, :] = mixed.astype(jnp.bfloat16)
-
-    for side in range(2):
-        for x in range(chips):
-            sib_copy(side, x).wait_send()
-        for step in range(1, chips):
-            far_copy(side, step).wait_send()
+
+        def add_up(t, carry):
+            sib_copy(side, chip, t).wait_recv()
+            summed = kept[side, t] + sib_in[side, chip, t].astype(jnp.float32)
+            for step in range(1, chips):
+                far_copy(side, step, t).wait_recv()
+                summed = summed + far_in[side, step - 1, t].astype(jnp.float32)
+            mixed[side, t] = summed.astype(jnp.bfloat16)
+            result_copy(side, t).start()
+            return carry
+
+        lax.fori_loop(0, out_tiles, add_up, 0)
+
+    def drain_out(t, carry):
+        for side in range(2):
+            result_copy(side, t).wait()
+            for x in range(chips):
+                sib_copy(side, x, t).wait_send()
+            for step in range(1, chips):
+                far_copy(side, step, t).wait_send()
+        return carry
+
+    lax.fori_loop(0, out_tiles, drain_out, 0)
 
     def drain(block, carry):
         @pl.when(has_right & (block <= c))
@@ -394,6 +403,20 @@
         return carry
 
     lax.fori_loop(0, 2 * n, drain, 0)
+
+
+def hand_over(source, target, sem):
+    part = source.shape[0] // 4
+    copies = [
+        pltpu.make_async_copy(
+            source.at[i * part : (i + 1) * part], target.at[i * part : (i + 1) * part], sem.at[i]
+        )
+        for i in range(4)
+    ]
+    for copy in copies:
+        copy.start()
+    for copy in copies:
+        copy.wait()
 
 
 def shards(n, n_head, tokens, lengths, q_weight, k_weight, v_weight, o_weight):
@@ -407,13 +430,14 @@
     bf16, f32 = jnp.bfloat16, jnp.float32
     dma = pltpu.SemaphoreType.DMA
     far = max(chips - 1, 1)
-    vmem = pl.BlockSpec(memory_space=pltpu.VMEM)
+    tile = min(256, width)
+    tiles = width // tile
     hbm = pl.BlockSpec(memory_space=pl.ANY)
-    return pl.pallas_call(
+    computed = pl.pallas_call(
         functools.partial(kernel, n, n_head),
         out_shape=jax.ShapeDtypeStruct((rows, width), bf16),
         in_specs=[pl.BlockSpec(memory_space=pltpu.SMEM)] + [hbm] * 5,
-        out_specs=vmem,
+        out_specs=hbm,
         scratch_shapes=[
             pltpu.VMEM((2, 1, group * half), jnp.int32),
             pltpu.VMEM((rows, HD), f32),
@@ -431,21 +455,29 @@
             pltpu.VMEM((2 * kv_heads, 1, group * half), f32),
             pltpu.VMEM((2 * kv_heads, HD, group * half), f32),
             pltpu.VMEM((half, q_cols), bf16),
-            pltpu.VMEM((half, width), f32),
-            pltpu.VMEM((2, half, width), f32),
-            pltpu.VMEM((2, chips, half, width), bf16),
-            pltpu.VMEM((2, chips, half, width), bf16),
-            pltpu.VMEM((2, far, half, width), bf16),
-            pltpu.VMEM((2, far, half, width), bf16),
+            pltpu.VMEM((2, tiles, half, tile), f32),
+            pltpu.VMEM((2, tiles, half, tile), bf16),
+            pltpu.VMEM((2, chips, tiles, half, tile), bf16),
+            pltpu.VMEM((2, chips, tiles, half, tile), bf16),
+            pltpu.VMEM((2, far, tiles, half, tile), bf16),
+            pltpu.VMEM((2, far, tiles, half, tile), bf16),
             dma((4,)), dma((4,)), dma((4,)), dma, dma,
             dma((2, 2, 2 * n)), dma((2, 2 * n)),
-            dma((2, chips)), dma((2, chips)),
-            dma((2, far)), dma((2, far)),
+            dma((2, chips, tiles)), dma((2, chips, tiles)),
+            dma((2, far, tiles)), dma((2, far, tiles)),
+            dma((2, tiles)),
         ],
         compiler_params=pltpu.CompilerParams(
             collective_id=0, has_side_effects=True, vmem_limit_bytes=60 * 2**20
         ),
     )(lengths, tokens, q_weight, k_weight, v_weight, o_weight)
+    return pl.pallas_call(
+        hand_over,
+        out_shape=jax.ShapeDtypeStruct((rows, width), bf16),
+        in_specs=[hbm],
+        out_specs=hbm,
+        scratch_shapes=[dma((4,))],
+    )(computed)
 
 
 def solution(mesh):

time: 67.1 us -> 91.6 us (1.37)
  the two profiles are of different devices: /device:TPU:0 before, /device:TPU:8 now
where the time goes in v3:
time: 91.6 us; the launch traced here: 91.4 us
  Pallas kernels  91.4 us (100%)
    pallas_call x1, Pallas kernels, shards(): pl.pallas_call(functools.partial(kernel, n, n_head), out_shape=jax.ShapeD...  58.5 us
    pallas_call x1, Pallas kernels, shards(): pl.pallas_call(hand_over, out_shape=jax.ShapeDtypeStruct((rows, width), b...  32.9 us

profile of v3, /device:TPU:8, one launch (start us, length us, event | category | flops | bytes accessed | tf_op | source)
XLA Modules:
  0.0 91.4 jit_solution(15888208030632503045)
XLA Ops:
  0.0 58.5 %shard_map.64.source = bf16[512,1024]{1,0:T(8,128)(2,1)} custom-call(s32[16]{0:T(128)} %lengths_ref.1, bf16[512,4096]{1,0:T(8,128)(2,1)} %tok_hbm.1, bf16[4096,1024]{1,0:T(8,128)(2,1)} %qw_hbm.1, bf16[4096,256]{1,0:T(8,128)(2,1)} %kw_hbm.1, bf16[4096,256]{1,0:T(8,128)(2,1)} %vw_hbm.1, bf16[1024,4096]{1,0:T(8,128)(2,1)} %ow_hbm.1), custom_call_target="tpu_custom_call" | custom-call | tf_op jit(solution)/shard_map/pallas_call | solution.py:436
  58.5 32.9 %shard_map.65 = bf16[512,1024]{1,0:T(8,128)(2,1)} custom-call(bf16[512,1024]{1,0:T(8,128)(2,1)} %shard_map.64.source), custom_call_target="tpu_custom_call" | custom-call | tf_op jit(solution)/shard_map/pallas_call | solution.py:474

commit v4 on v3

--- a/solution.py
+++ b/solution.py
@@ -68,9 +68,12 @@
     def greet(target):
         pl.semaphore_signal(barrier, inc=1, device_id=target, device_id_type=MESH)
 
-    @pl.when(has_left)
-    def _():
-        greet({"ctx": c - 1})
+    reaches = range(1, n, 2)
+    for reach in reaches:
+
+        @pl.when(c >= reach)
+        def _():
+            greet({"ctx": c - reach})
 
     @pl.when(has_right)
     def _():
@@ -138,7 +141,7 @@
             values[block, g] = raw.T.astype(jnp.bfloat16)
 
     def block_copies(block, way):
-        target = {"ctx": c + 1 if way else c - 1}
+        target = {"ctx": c + 2 * way - 1}
         return [
             pltpu.make_async_remote_copy(
                 src_ref=ref.at[block],
@@ -164,16 +167,20 @@
             def _():
                 onward[kind].start()
 
-    greeted = 1 + (chips - 1) + has_left.astype(jnp.int32) + has_right.astype(jnp.int32)
+    greeted = 1 + (chips - 1) + has_left.astype(jnp.int32)
+    for reach in reaches:
+        greeted = greeted + (c + reach < n).astype(jnp.int32)
     pl.semaphore_wait(barrier, greeted)
-
-    @pl.when(has_right)
-    def _():
-        send(low_block, 1)
 
     @pl.when(has_left)
     def _():
         send(high_block, 0)
+
+    for reach in reaches:
+
+        @pl.when(c + reach < n)
+        def _():
+            send(low_block, (reach + 1) // 2)
 
     load_q.wait()
     factor = math.log2(math.e) / math.sqrt(HD)
@@ -298,20 +305,18 @@
     def from_right(i):
         return (i >= 1) & (i <= right_count)
 
-    def passes_right(i):
-        return from_left(i) & has_right
-
     def passes_left(i):
         return from_right(i) & has_left & (2 * n - 1 - c - i >= n - c)
 
     last_pass = jnp.where(has_left, jnp.minimum(right_count, n - 1), 0)
     finish_turn = jnp.maximum(c, jnp.where(c < n - c, last_pass, right_count) - 1)
 
-    def arrive(i):
+    def arrive_left(i):
         @pl.when(from_left(i))
         def _():
-            receive(c - i, has_right, 1)
-
+            receive(c - i, has_right & (i % 2 == 1), 1)
+
+    def arrive_right(i):
         @pl.when(from_right(i))
         def _():
             receive(2 * n - 1 - c - i, passes_left(i), 0)
@@ -320,14 +325,12 @@
         def _():
             send(low_block, 0)
 
-    arrive(0)
+    arrive_right(0)
 
     def turn(i, carry):
-        early = passes_right(i + 1) | passes_left(i + 1)
-
-        @pl.when(early)
-        def _():
-            arrive(i + 1)
+        @pl.when(passes_left(i + 1))
+        def _():
+            arrive_right(i + 1)
 
         @pl.when(i == 0)
         def _():
@@ -350,9 +353,11 @@
         def _():
             attend(1, 2 * n - 1 - c - i, False)
 
-        @pl.when(jnp.logical_not(early))
-        def _():
-            arrive(i + 1)
+        @pl.when(jnp.logical_not(passes_left(i + 1)))
+        def _():
+            arrive_right(i + 1)
+
+        arrive_left(i + 1)
 
         return carry
 
@@ -390,7 +395,7 @@
     lax.fori_loop(0, out_tiles, drain_out, 0)
 
     def drain(block, carry):
-        @pl.when(has_right & (block <= c))
+        @pl.when(has_right & ((block == c) | ((block < c) & ((c - block) % 2 == 1))))
         def _():
             for copy in block_copies(block, 1):
                 copy.wait_send()
@@ -403,20 +408,16 @@
         return carry
 
     lax.fori_loop(0, 2 * n, drain, 0)
-
-
-def hand_over(source, target, sem):
-    part = source.shape[0] // 4
-    copies = [
-        pltpu.make_async_copy(
-            source.at[i * part : (i + 1) * part], target.at[i * part : (i + 1) * part], sem.at[i]
-        )
-        for i in range(4)
-    ]
-    for copy in copies:
-        copy.start()
-    for copy in copies:
-        copy.wait()
+    for reach in reaches[1:]:
+
+        @pl.when(c + reach < n)
+        def _():
+            for copy in block_copies(low_block, (reach + 1) // 2):
+                copy.wait_send()
+
+
+def hand_over(source, target):
+    target[...] = source[...]
 
 
 def shards(n, n_head, tokens, lengths, q_weight, k_weight, v_weight, o_weight):
@@ -462,7 +463,7 @@
             pltpu.VMEM((2, far, tiles, half, tile), bf16),
             pltpu.VMEM((2, far, tiles, half, tile), bf16),
             dma((4,)), dma((4,)), dma((4,)), dma, dma,
-            dma((2, 2, 2 * n)), dma((2, 2 * n)),
+            dma((1 + n // 2, 2, 2 * n)), dma((2, 2 * n)),
             dma((2, chips, tiles)), dma((2, chips, tiles)),
             dma((2, far, tiles)), dma((2, far, tiles)),
             dma((2, tiles)),
@@ -474,9 +475,9 @@
     return pl.pallas_call(
         hand_over,
         out_shape=jax.ShapeDtypeStruct((rows, width), bf16),
-        in_specs=[hbm],
-        out_specs=hbm,
-        scratch_shapes=[dma((4,))],
+        grid=(4,),
+        in_specs=[pl.BlockSpec((rows // 4, width), lambda i: (i, 0))],
+        out_specs=pl.BlockSpec((rows // 4, width), lambda i: (i, 0)),
     )(computed)
 
 

time: 91.6 us -> 62.2 us (0.68)
  the two profiles are of different devices: /device:TPU:8 before, /device:TPU:24 now
where the time goes in v4:
time: 62.2 us; the launch traced here: 62 us
  Pallas kernels  62 us (100%)
    pallas_call x1, Pallas kernels, shards(): pl.pallas_call(functools.partial(kernel, n, n_head), out_shape=jax.ShapeD...  58.6 us
    pallas_call x1, Pallas kernels, shards(): pl.pallas_call(hand_over, out_shape=jax.ShapeDtypeStruct((rows, width), b...  3.37 us

profile of v4, /device:TPU:24, one launch (start us, length us, event | category | flops | bytes accessed | tf_op | source)
XLA Modules:
  0.0 62.0 jit_solution(481545138109873519)
XLA Ops:
  0.0 58.6 %shard_map.64.source = bf16[512,1024]{1,0:T(8,128)(2,1)} custom-call(s32[16]{0:T(128)} %lengths_ref.1, bf16[512,4096]{1,0:T(8,128)(2,1)} %tok_hbm.1, bf16[4096,1024]{1,0:T(8,128)(2,1)} %qw_hbm.1, bf16[4096,256]{1,0:T(8,128)(2,1)} %kw_hbm.1, bf16[4096,256]{1,0:T(8,128)(2,1)} %vw_hbm.1, bf16[1024,4096]{1,0:T(8,128)(2,1)} %ow_hbm.1), custom_call_target="tpu_custom_call" | custom-call | tf_op jit(solution)/shard_map/pallas_call | solution.py:437
  58.6 3.4 %shard_map.65 = bf16[512,1024]{1,0:T(8,128)(2,1)} custom-call(bf16[512,1024]{1,0:T(8,128)(2,1)} %shard_map.64.source), custom_call_target="tpu_custom_call" | custom-call | tf_op jit(solution)/shard_map/pallas_call | solution.py:475

commit v5 on v4

--- a/solution.py
+++ b/solution.py
@@ -19,9 +19,9 @@
 
 def kernel(
     n, n_head, lengths_ref, tok_hbm, qw_hbm, kw_hbm, vw_hbm, ow_hbm,
-    out_ref,
+    near_ref, far_ref,
     first_ref, cos_ref, sin_ref, tok, qw, kvw, ow, kv_acc, norm, query, keys, values, top, total, accum, attended,
-    kept, mixed, sib_out, sib_in, far_out, far_in,
+    kept, near, sib_out, sib_in, far_out,
     tok_sem, kw_sem, vw_sem, qw_sem, ow_sem,
     kv_send, kv_recv, sib_send, sib_recv, far_send, far_recv, out_sem,
 ):
@@ -33,7 +33,7 @@
     wide_rows = group * half
     k_cols = kv_heads * HD
     chips = n_head // 2
-    width = out_ref.shape[1]
+    width = near_ref.shape[1]
     pieces = 4
     piece = depth // pieces
 
@@ -115,6 +115,11 @@
     def project_piece(k, carry):
         for copy in load_piece(k):
             copy.wait()
+
+        @pl.when(k == pieces // 2)
+        def _():
+            load_q.start()
+
         cols = pl.ds(pl.multiple_of(k * piece, piece), piece)
 
         kv_acc[...] += jnp.dot(tok[:, cols], kvw[cols, :], preferred_element_type=jnp.float32)
@@ -128,8 +133,6 @@
         return carry
 
     lax.fori_loop(0, pieces, project_piece, 0)
-    load_q.start()
-    load_o.start()
     mean = jnp.sum(norm[...], axis=1, keepdims=True) * (1.0 / depth)
     norm[...] = jnp.broadcast_to(lax.rsqrt(mean + 1e-05), norm.shape)
     for g in range(kv_heads):
@@ -183,6 +186,7 @@
             send(low_block, (reach + 1) // 2)
 
     load_q.wait()
+    load_o.start()
     factor = math.log2(math.e) / math.sqrt(HD)
     tile = min(256, q_heads * HD)
 
@@ -244,11 +248,15 @@
             device_id_type=MESH,
         )
 
+    def tile_of(side, t):
+        cols = pl.ds(pl.multiple_of(t * out_tile, out_tile), out_tile)
+        return pl.ds(side * half, half), cols
+
     def far_copy(side, step, t):
         x = other_chip(step)
         return pltpu.make_async_remote_copy(
             src_ref=far_out.at[side, step - 1, t],
-            dst_ref=far_in.at[side, step - 1, t],
+            dst_ref=far_ref.at[step - 1, *tile_of(side, t)],
             send_sem=far_send.at[side, step - 1, t],
             recv_sem=far_recv.at[side, step - 1, t],
             device_id={"head": x * 2 + core},
@@ -321,11 +329,11 @@
         def _():
             receive(2 * n - 1 - c - i, passes_left(i), 0)
 
-        @pl.when((i == right_count) & has_left & (c >= n - c))
-        def _():
-            send(low_block, 0)
-
-    arrive_right(0)
+    sends_low = has_left & (c >= n - c)
+
+    @pl.when(sends_low & (right_count == 0))
+    def _():
+        send(low_block, 0)
 
     def turn(i, carry):
         @pl.when(passes_left(i + 1))
@@ -345,7 +353,7 @@
         def _():
             finish(0)
 
-        @pl.when((i <= c) & (c - i >= n - 1 - c))
+        @pl.when((i <= c) & (c - i >= n - 1 - c) & (has_right | (i == 0)))
         def _():
             attend(1, c - i, False)
 
@@ -357,39 +365,48 @@
         def _():
             arrive_right(i + 1)
 
+        @pl.when(sends_low & (i + 1 == right_count))
+        def _():
+            send(low_block, 0)
+
         arrive_left(i + 1)
-
         return carry
 
     lax.fori_loop(0, n + 1, turn, 0)
+
+    @pl.when(jnp.logical_not(has_right))
+    def _():
+        def put_off(block, carry):
+            attend(1, block, False)
+            return carry
+
+        lax.fori_loop(0, n - 1, put_off, 0)
+
     finish(1)
 
-    def result_copy(side, t):
-        cols = pl.ds(pl.multiple_of(t * out_tile, out_tile), out_tile)
-        at = slice(side * half, (side + 1) * half)
-        return pltpu.make_async_copy(mixed.at[side, t], out_ref.at[at, cols], out_sem.at[side, t])
+    def near_copy(side, t):
+        return pltpu.make_async_copy(
+            near.at[side, t], near_ref.at[*tile_of(side, t)], out_sem.at[side, t]
+        )
 
     for side in range(2):
 
         def add_up(t, carry):
             sib_copy(side, chip, t).wait_recv()
             summed = kept[side, t] + sib_in[side, chip, t].astype(jnp.float32)
-            for step in range(1, chips):
-                far_copy(side, step, t).wait_recv()
-                summed = summed + far_in[side, step - 1, t].astype(jnp.float32)
-            mixed[side, t] = summed.astype(jnp.bfloat16)
-            result_copy(side, t).start()
+            near[side, t] = summed.astype(jnp.bfloat16)
+            near_copy(side, t).start()
             return carry
 
         lax.fori_loop(0, out_tiles, add_up, 0)
 
     def drain_out(t, carry):
         for side in range(2):
-            result_copy(side, t).wait()
+            near_copy(side, t).wait()
             for x in range(chips):
                 sib_copy(side, x, t).wait_send()
             for step in range(1, chips):
-                far_copy(side, step, t).wait_send()
+                far_copy(side, step, t).wait()
         return carry
 
     lax.fori_loop(0, out_tiles, drain_out, 0)
@@ -414,10 +431,6 @@
         def _():
             for copy in block_copies(low_block, (reach + 1) // 2):
                 copy.wait_send()
-
-
-def hand_over(source, target):
-    target[...] = source[...]
 
 
 def shards(n, n_head, tokens, lengths, q_weight, k_weight, v_weight, o_weight):
@@ -434,11 +447,14 @@
     tile = min(256, width)
     tiles = width // tile
     hbm = pl.BlockSpec(memory_space=pl.ANY)
-    computed = pl.pallas_call(
+    near, others = pl.pallas_call(
         functools.partial(kernel, n, n_head),
-        out_shape=jax.ShapeDtypeStruct((rows, width), bf16),
+        out_shape=(
+            jax.ShapeDtypeStruct((rows, width), bf16),
+            jax.ShapeDtypeStruct((far, rows, width), bf16),
+        ),
         in_specs=[pl.BlockSpec(memory_space=pltpu.SMEM)] + [hbm] * 5,
-        out_specs=hbm,
+        out_specs=(hbm, hbm),
         scratch_shapes=[
             pltpu.VMEM((2, 1, group * half), jnp.int32),
             pltpu.VMEM((rows, HD), f32),
@@ -461,7 +477,6 @@
             pltpu.VMEM((2, chips, tiles, half, tile), bf16),
             pltpu.VMEM((2, chips, tiles, half, tile), bf16),
             pltpu.VMEM((2, far, tiles, half, tile), bf16),
-            pltpu.VMEM((2, far, tiles, half, tile), bf16),
             dma((4,)), dma((4,)), dma((4,)), dma, dma,
             dma((1 + n // 2, 2, 2 * n)), dma((2, 2 * n)),
             dma((2, chips, tiles)), dma((2, chips, tiles)),
@@ -472,13 +487,10 @@
             collective_id=0, has_side_effects=True, vmem_limit_bytes=60 * 2**20
         ),
     )(lengths, tokens, q_weight, k_weight, v_weight, o_weight)
-    return pl.pallas_call(
-        hand_over,
-        out_shape=jax.ShapeDtypeStruct((rows, width), bf16),
-        grid=(4,),
-        in_specs=[pl.BlockSpec((rows // 4, width), lambda i: (i, 0))],
-        out_specs=pl.BlockSpec((rows // 4, width), lambda i: (i, 0)),
-    )(computed)
+    mixed = near.astype(f32)
+    for step in range(chips - 1):
+        mixed = mixed + others[step].astype(f32)
+    return mixed.astype(bf16)
 
 
 def solution(mesh):

time: 62.2 us -> 59.4 us (0.955)
  Pallas kernels: 62 us -> 56.2 us
  other arithmetic: 0 us -> 2.91 us
    pallas_call x2 -> x1, Pallas kernels: 62 us -> 56.2 us  [shards(): pl.pallas_call(functools.partial(kernel, n, n_head), out_shape=(jax.Shape...]
    convert_element_type x0 -> x1, other arithmetic: none -> 2.91 us  [shards(): return mixed.astype(bf16)]
where the time goes in v5:
time: 59.4 us; the launch traced here: 59.2 us
  Pallas kernels  56.2 us (95%)
  other arithmetic  2.91 us (5%)
    pallas_call x1, Pallas kernels, shards(): pl.pallas_call(functools.partial(kernel, n, n_head), out_shape=(jax.Shape...  56.2 us
    convert_element_type x1, other arithmetic, shards(): return mixed.astype(bf16)  2.91 us

profile of v5, /device:TPU:24, one launch (start us, length us, event | category | flops | bytes accessed | tf_op | source)
XLA Modules:
  0.0 59.2 jit_solution(3691686510381016650)
XLA Ops:
  0.0 56.2 %shard_map.64 = (bf16[512,1024]{1,0:T(8,128)(2,1)}, bf16[1,512,1024]{2,1,0:T(8,128)(2,1)}) custom-call(s32[16]{0:T(128)} %lengths_ref.1, bf16[512,4096]{1,0:T(8,128)(2,1)} %tok_hbm.1, bf16[4096,1024]{1,0:T(8,128)(2,1)} %qw_hbm.1, bf16[4096,256]{1,0:T(8,128)(2,1)} %kw_hbm.1, bf16[4096,256]{1,0:T(8,128)(2,1)} %vw_hbm.1, bf16[1024,4096]{1,0:T(8,128)(2,1)} %ow_hbm.1), custom_call_target="tpu_custom_call" | custom-call | tf_op jit(solution)/shard_map/pallas_call | solution.py:450
  56.3 2.9 %fusion = bf16[512,1024]{1,0:T(8,128)(2,1)} fusion(bf16[512,1024]{1,0:T(8,128)(2,1)} %get-tuple-element.7, bf16[1,512,1024]{2,1,0:T(8,128)(2,1)} %get-tuple-element.8), kind=kLoop, calls=%fused_computation.1 | loop fusion | flops 2097152 | bytes 3145728 | tf_op jit(solution)/shard_map/convert_element_type | solution.py:493

commit v6 on v5

--- a/solution.py
+++ b/solution.py
@@ -21,9 +21,9 @@
     n, n_head, lengths_ref, tok_hbm, qw_hbm, kw_hbm, vw_hbm, ow_hbm,
     near_ref, far_ref,
     first_ref, cos_ref, sin_ref, tok, qw, kvw, ow, kv_acc, norm, query, keys, values, top, total, accum, attended,
-    kept, near, sib_out, sib_in, far_out,
+    kept, sib_out, sib_in, far_out,
     tok_sem, kw_sem, vw_sem, qw_sem, ow_sem,
-    kv_send, kv_recv, sib_send, sib_recv, far_send, far_recv, out_sem,
+    kv_send, kv_recv, sib_send, sib_recv, far_send, far_recv,
 ):
     rows, depth = tok.shape
     half = rows // 2
@@ -68,12 +68,9 @@
     def greet(target):
         pl.semaphore_signal(barrier, inc=1, device_id=target, device_id_type=MESH)
 
-    reaches = range(1, n, 2)
-    for reach in reaches:
-
-        @pl.when(c >= reach)
-        def _():
-            greet({"ctx": c - reach})
+    @pl.when(has_left)
+    def _():
+        greet({"ctx": c - 1})
 
     @pl.when(has_right)
     def _():
@@ -170,20 +167,16 @@
             def _():
                 onward[kind].start()
 
-    greeted = 1 + (chips - 1) + has_left.astype(jnp.int32)
-    for reach in reaches:
-        greeted = greeted + (c + reach < n).astype(jnp.int32)
+    greeted = 1 + (chips - 1) + has_left.astype(jnp.int32) + has_right.astype(jnp.int32)
     pl.semaphore_wait(barrier, greeted)
 
     @pl.when(has_left)
     def _():
         send(high_block, 0)
 
-    for reach in reaches:
-
-        @pl.when(c + reach < n)
-        def _():
-            send(low_block, (reach + 1) // 2)
+    @pl.when(has_right)
+    def _():
+        send(low_block, 1)
 
     load_q.wait()
     load_o.start()
@@ -322,7 +315,7 @@
     def arrive_left(i):
         @pl.when(from_left(i))
         def _():
-            receive(c - i, has_right & (i % 2 == 1), 1)
+            receive(c - i, has_right, 1)
 
     def arrive_right(i):
         @pl.when(from_right(i))
@@ -340,6 +333,10 @@
         def _():
             arrive_right(i + 1)
 
+        @pl.when(from_left(i + 1) & has_right)
+        def _():
+            arrive_left(i + 1)
+
         @pl.when(i == 0)
         def _():
             attend(0, low_block, True)
@@ -369,7 +366,10 @@
         def _():
             send(low_block, 0)
 
-        arrive_left(i + 1)
+        @pl.when(jnp.logical_not(has_right))
+        def _():
+            arrive_left(i + 1)
+
         return carry
 
     lax.fori_loop(0, n + 1, turn, 0)
@@ -384,25 +384,18 @@
 
     finish(1)
 
-    def near_copy(side, t):
-        return pltpu.make_async_copy(
-            near.at[side, t], near_ref.at[*tile_of(side, t)], out_sem.at[side, t]
-        )
-
     for side in range(2):
 
         def add_up(t, carry):
             sib_copy(side, chip, t).wait_recv()
             summed = kept[side, t] + sib_in[side, chip, t].astype(jnp.float32)
-            near[side, t] = summed.astype(jnp.bfloat16)
-            near_copy(side, t).start()
+            near_ref[tile_of(side, t)] = summed.astype(jnp.bfloat16)
             return carry
 
         lax.fori_loop(0, out_tiles, add_up, 0)
 
     def drain_out(t, carry):
         for side in range(2):
-            near_copy(side, t).wait()
             for x in range(chips):
                 sib_copy(side, x, t).wait_send()
             for step in range(1, chips):
@@ -412,7 +405,7 @@
     lax.fori_loop(0, out_tiles, drain_out, 0)
 
     def drain(block, carry):
-        @pl.when(has_right & ((block == c) | ((block < c) & ((c - block) % 2 == 1))))
+        @pl.when(has_right & (block <= c))
         def _():
             for copy in block_copies(block, 1):
                 copy.wait_send()
@@ -425,12 +418,6 @@
         return carry
 
     lax.fori_loop(0, 2 * n, drain, 0)
-    for reach in reaches[1:]:
-
-        @pl.when(c + reach < n)
-        def _():
-            for copy in block_copies(low_block, (reach + 1) // 2):
-                copy.wait_send()
 
 
 def shards(n, n_head, tokens, lengths, q_weight, k_weight, v_weight, o_weight):
@@ -447,14 +434,15 @@
     tile = min(256, width)
     tiles = width // tile
     hbm = pl.BlockSpec(memory_space=pl.ANY)
+    vmem = pl.BlockSpec(memory_space=pltpu.VMEM)
     near, others = pl.pallas_call(
         functools.partial(kernel, n, n_head),
         out_shape=(
-            jax.ShapeDtypeStruct((rows, width), bf16),
-            jax.ShapeDtypeStruct((far, rows, width), bf16),
+            pltpu.VMEM((rows, width), bf16),
+            pltpu.VMEM((far, rows, width), bf16),
         ),
         in_specs=[pl.BlockSpec(memory_space=pltpu.SMEM)] + [hbm] * 5,
-        out_specs=(hbm, hbm),
+        out_specs=(vmem, vmem),
         scratch_shapes=[
             pltpu.VMEM((2, 1, group * half), jnp.int32),
             pltpu.VMEM((rows, HD), f32),
@@ -473,18 +461,16 @@
             pltpu.VMEM((2 * kv_heads, HD, group * half), f32),
             pltpu.VMEM((half, q_cols), bf16),
             pltpu.VMEM((2, tiles, half, tile), f32),
-            pltpu.VMEM((2, tiles, half, tile), bf16),
             pltpu.VMEM((2, chips, tiles, half, tile), bf16),
             pltpu.VMEM((2, chips, tiles, half, tile), bf16),
             pltpu.VMEM((2, far, tiles, half, tile), bf16),
             dma((4,)), dma((4,)), dma((4,)), dma, dma,
-            dma((1 + n // 2, 2, 2 * n)), dma((2, 2 * n)),
+            dma((2, 2, 2 * n)), dma((2, 2 * n)),
             dma((2, chips, tiles)), dma((2, chips, tiles)),
             dma((2, far, tiles)), dma((2, far, tiles)),
-            dma((2, tiles)),
         ],
         compiler_params=pltpu.CompilerParams(
-            collective_id=0, has_side_effects=True, vmem_limit_bytes=60 * 2**20
+            collective_id=0, has_side_effects=True, vmem_limit_bytes=56 * 2**20
         ),
     )(lengths, tokens, q_weight, k_weight, v_weight, o_weight)
     mixed = near.astype(f32)

time: 59.4 us -> 58.3 us (0.981)
  other arithmetic: 2.91 us -> 1.37 us
    convert_element_type x1, other arithmetic: 2.91 us -> 1.37 us  [shards(): return mixed.astype(bf16)]
where the time goes in v6:
time: 58.3 us; the launch traced here: 58.1 us
  Pallas kernels  56.7 us (97%)
  other arithmetic  1.37 us (2%)
    pallas_call x1, Pallas kernels, shards(): pl.pallas_call(functools.partial(kernel, n, n_head), out_shape=(pltpu.VME...  56.7 us
    convert_element_type x1, other arithmetic, shards(): return mixed.astype(bf16)  1.37 us

profile of v6, /device:TPU:24, one launch (start us, length us, event | category | flops | bytes accessed | tf_op | source)
XLA Modules:
  0.0 58.1 jit_solution(15873122001326364346)
XLA Ops:
  0.0 56.7 %shard_map.64 = (bf16[512,1024]{1,0:T(8,128)(2,1)S(1)}, bf16[1,512,1024]{2,1,0:T(8,128)(2,1)S(1)}) custom-call(s32[16]{0:T(128)} %lengths_ref.1, bf16[512,4096]{1,0:T(8,128)(2,1)} %tok_hbm.1, bf16[4096,1024]{1,0:T(8,128)(2,1)} %qw_hbm.1, bf16[4096,256]{1,0:T(8,128)(2,1)} %kw_hbm.1, bf16[4096,256]{1,0:T(8,128)(2,1)} %vw_hbm.1, bf16[1024,4096]{1,0:T(8,128)(2,1)} %ow_hbm.1), custom_call_target="tpu_custom_call" | custom-call | tf_op jit(solution)/shard_map/pallas_call | solution.py:438
  56.8 1.4 %fusion = bf16[512,1024]{1,0:T(8,128)(2,1)} fusion(bf16[512,1024]{1,0:T(8,128)(2,1)S(1)} %get-tuple-element.7, bf16[1,512,1024]{2,1,0:T(8,128)(2,1)S(1)} %get-tuple-element.8), kind=kLoop, calls=%fused_computation.1 | loop fusion | flops 2097152 | bytes 3145728 | tf_op jit(solution)/shard_map/convert_element_type | solution.py:479

commit v7 on v6

--- a/solution.py
+++ b/solution.py
@@ -109,32 +109,35 @@
     kv_acc[...] = jnp.zeros_like(kv_acc)
     norm[...] = jnp.zeros_like(norm)
 
-    def project_piece(k, carry):
-        for copy in load_piece(k):
-            copy.wait()
-
-        @pl.when(k == pieces // 2)
-        def _():
-            load_q.start()
-
-        cols = pl.ds(pl.multiple_of(k * piece, piece), piece)
-
-        kv_acc[...] += jnp.dot(tok[:, cols], kvw[cols, :], preferred_element_type=jnp.float32)
-        for r in range(0, rows, 64):
-            wide = tok[r : r + 64, cols].astype(jnp.float32)
-            sq = wide * wide
-            part = sq[:, 0:HD]
-            for s in range(1, piece // HD):
-                part = part + sq[:, s * HD : (s + 1) * HD]
-            norm[r : r + 64, :] += part
-        return carry
-
-    lax.fori_loop(0, pieces, project_piece, 0)
-    mean = jnp.sum(norm[...], axis=1, keepdims=True) * (1.0 / depth)
-    norm[...] = jnp.broadcast_to(lax.rsqrt(mean + 1e-05), norm.shape)
-    for g in range(kv_heads):
-        for side, block in ((0, low_block), (1, high_block)):
-            at = slice(side * half, (side + 1) * half)
+    def project_side(side, block):
+        at = slice(side * half, (side + 1) * half)
+
+        def project_piece(k, carry):
+            if side == 0:
+                for copy in load_piece(k):
+                    copy.wait()
+
+                @pl.when(k == pieces // 2)
+                def _():
+                    load_q.start()
+
+            cols = pl.ds(pl.multiple_of(k * piece, piece), piece)
+            kv_acc[at, :] += jnp.dot(
+                tok[at, cols], kvw[cols, :], preferred_element_type=jnp.float32
+            )
+            for r in range(side * half, (side + 1) * half, 64):
+                wide = tok[r : r + 64, cols].astype(jnp.float32)
+                sq = wide * wide
+                part = sq[:, 0:HD]
+                for s in range(1, piece // HD):
+                    part = part + sq[:, s * HD : (s + 1) * HD]
+                norm[r : r + 64, :] += part
+            return carry
+
+        lax.fori_loop(0, pieces, project_piece, 0)
+        mean = jnp.sum(norm[at, :], axis=1, keepdims=True) * (1.0 / depth)
+        norm[at, :] = jnp.broadcast_to(lax.rsqrt(mean + 1e-05), (half, HD))
+        for g in range(kv_heads):
             raw = kv_acc[at, g * HD : (g + 1) * HD] * norm[at, :]
             keys[block, g] = rotated(raw, cos_ref[at, :], sin_ref[at, :]).astype(jnp.bfloat16)
             raw = kv_acc[at, k_cols + g * HD : k_cols + (g + 1) * HD] * norm[at, :]
@@ -168,15 +171,19 @@
                 onward[kind].start()
 
     greeted = 1 + (chips - 1) + has_left.astype(jnp.int32) + has_right.astype(jnp.int32)
+
+    project_side(0, low_block)
     pl.semaphore_wait(barrier, greeted)
+
+    @pl.when(has_right)
+    def _():
+        send(low_block, 1)
+
+    project_side(1, high_block)
 
     @pl.when(has_left)
     def _():
         send(high_block, 0)
-
-    @pl.when(has_right)
-    def _():
-        send(low_block, 1)
 
     load_q.wait()
     load_o.start()

time: 58.3 us -> 58.2 us (level)
  no operation moved by 1% of the time
where the time goes in v7:
time: 58.2 us; the launch traced here: 58 us
  Pallas kernels  56.6 us (97%)
  other arithmetic  1.37 us (2%)
    pallas_call x1, Pallas kernels, shards(): pl.pallas_call(functools.partial(kernel, n, n_head), out_shape=(pltpu.VME...  56.6 us
    convert_element_type x1, other arithmetic, shards(): return mixed.astype(bf16)  1.37 us

profile of v7, /device:TPU:24, one launch (start us, length us, event | category | flops | bytes accessed | tf_op | source)
XLA Modules:
  0.0 58.0 jit_solution(1035013156519269527)
XLA Ops:
  0.0 56.6 %shard_map.64 = (bf16[512,1024]{1,0:T(8,128)(2,1)S(1)}, bf16[1,512,1024]{2,1,0:T(8,128)(2,1)S(1)}) custom-call(s32[16]{0:T(128)} %lengths_ref.1, bf16[512,4096]{1,0:T(8,128)(2,1)} %tok_hbm.1, bf16[4096,1024]{1,0:T(8,128)(2,1)} %qw_hbm.1, bf16[4096,256]{1,0:T(8,128)(2,1)} %kw_hbm.1, bf16[4096,256]{1,0:T(8,128)(2,1)} %vw_hbm.1, bf16[1024,4096]{1,0:T(8,128)(2,1)} %ow_hbm.1), custom_call_target="tpu_custom_call" | custom-call | tf_op jit(solution)/shard_map/pallas_call | solution.py:445
  56.6 1.4 %fusion = bf16[512,1024]{1,0:T(8,128)(2,1)} fusion(bf16[512,1024]{1,0:T(8,128)(2,1)S(1)} %get-tuple-element.7, bf16[1,512,1024]{2,1,0:T(8,128)(2,1)S(1)} %get-tuple-element.8), kind=kLoop, calls=%fused_computation.1 | loop fusion | flops 2097152 | bytes 3145728 | tf_op jit(solution)/shard_map/convert_element_type | solution.py:486
